TPU v7x, 32 devices: a whole 2x2x4 slice. The times are simulated.
32 devices in a mesh: grp: 16 (over z, y, x), head: 2 (over core).
Axes of the slice: x: 2, y: 2, z: 4, core: 2. Of those that a mesh axis runs over, the one named last changes fastest.
Arguments:
- residual: bfloat16 [256, 2880], P('grp'), may hold values from -4 to 4
- queries: bfloat16 [256, 8, 256], P('grp', 'head'), may hold values from -200 to 200
- kv_cache: bfloat16 [256, 8, 128, 128], P('grp', 'head'), may hold values from -5 to 5
- new_kv: bfloat16 [256, 8, 128], P('grp', 'head'), may hold values from -5 to 5
- positions: int32 [256], P('grp'), may hold values from 0 to 383
- sink_logits: float32 [8, 4], P('head'), may hold values from 0 to 5
- out_proj: bfloat16 [8, 256, 2880], P('head'), may hold values from -0.375 to 0.375
- norm_gain: float32 [2880], replicated, may hold values from 0.5 to 1.5
- route_ids: int32 [256, 4], P('grp'), may hold values from 0 to 15, all different within a row; in each aligned block of 16 rows (0 to 15, 16 to 31, ...) at most 4 rows name the same one
- route_weights: int32 [256, 4], P('grp'), may hold values from 1 to 65535
- w_gate_up: bfloat16 [16, 2880, 2880], P('grp', None, 'head'), may hold values from -0.109375 to 0.109375
- w_down: bfloat16 [16, 1440, 2880], P('grp', 'head'), may hold values from -0.15625 to 0.15625
Outputs:
- layer_out: bfloat16 [256, 2880], P('grp', 'head')
Inputs may be any that keep to these rules, and one draw needn't show every extreme that they name: `route_ids`: in the 16 rows of one index of grp, at most 4 rows name the same expert; each row names 4 different experts.
All inputs are finite; a program needn't handle non-finite values.
Results may differ from a plain program's by a relative error of at most 0.025.
Values may be sent and summed in bfloat16 or wider, within the bound.
A program may use at most 64 MiB of HBM per device.

v0:
```python
import jax
import jax.numpy as jnp
from jax import lax
from jax.sharding import PartitionSpec as P

epsilon = 1e-05
swish_alpha = 1.702


def rms_norm(values, gain):
    as_float = values.astype(jnp.float32)
    mean_square = jnp.mean(as_float * as_float, axis=-1, keepdims=True)
    return (as_float * lax.rsqrt(mean_square + epsilon) * gain).astype(jnp.bfloat16)


def attend(queries, kv_cache, new_kv, positions, sink_logits):
    head_dim = new_kv.shape[2] // 2
    window = kv_cache.shape[2]
    row_count = queries.shape[0]
    kv_heads = queries.shape[1]
    groups = queries.shape[2] // head_dim
    slot_iota = jnp.arange(window, dtype=jnp.int32)
    current = positions % window
    slot_lag = (positions[:, None] - slot_iota[None, :]) % window
    is_valid = slot_lag <= positions[:, None]
    is_new = slot_iota[None, :] == current[:, None]
    merged = jnp.where(is_new[:, None, :, None], new_kv[:, :, None, :], kv_cache)
    key_part = merged[..., :head_dim]
    value_part = merged[..., head_dim:]
    query_part = queries.reshape(row_count, kv_heads, groups, head_dim)
    scores = jnp.einsum(
        "thgd,thwd->thgw", query_part, key_part, preferred_element_type=jnp.float32
    ) * head_dim ** (-0.5)
    scores = jnp.where(is_valid[:, None, None, :], scores, -jnp.inf)
    sink_col = sink_logits[None, :, :, None]
    largest = jnp.maximum(jnp.max(scores, axis=-1, keepdims=True), sink_col)
    weights_exp = jnp.exp(scores - largest)
    denominator = jnp.sum(weights_exp, axis=-1, keepdims=True) + jnp.exp(sink_col - largest)
    weights = (weights_exp / denominator).astype(jnp.bfloat16)
    mixed = jnp.einsum(
        "thgw,thwd->thgd", weights, value_part, preferred_element_type=jnp.float32
    ).astype(jnp.bfloat16)
    return mixed.reshape(row_count, kv_heads * groups * head_dim)


def local(
    residual,
    queries,
    kv_cache,
    new_kv,
    positions,
    sink_logits,
    out_proj,
    norm_gain,
    route_ids,
    route_weights,
    w_gate_up,
    w_down,
):
    row_count = residual.shape[0]
    width_all = out_proj.shape[2]
    share_width = width_all // lax.axis_size("head")
    share_start = lax.axis_index("head") * share_width
    mixed = attend(queries, kv_cache, new_kv, positions, sink_logits)
    partial_value = jnp.dot(
        mixed, out_proj.reshape(-1, width_all), preferred_element_type=jnp.float32
    )
    attention = lax.psum(partial_value.astype(jnp.bfloat16), "head").astype(jnp.float32)
    hidden_full = (residual.astype(jnp.float32) + attention).astype(jnp.bfloat16)
    sent_rows = rms_norm(hidden_full, norm_gain)
    hidden_here = lax.dynamic_slice_in_dim(hidden_full, share_start, share_width, 1)
    expert_count = lax.axis_size("grp")
    topk_count = route_ids.shape[1]
    capacity = max(2, row_count * topk_count // expert_count)
    flat_ids = route_ids.reshape(-1)
    assign_iota = jnp.arange(flat_ids.shape[0], dtype=jnp.int32)
    earlier = (flat_ids[:, None] == flat_ids[None, :]) & (
        assign_iota[:, None] > assign_iota[None, :]
    )
    slot_rank = jnp.sum(earlier.astype(jnp.int32), axis=1)
    slot_dest = flat_ids * capacity + slot_rank
    slot_iota = jnp.arange(expert_count * capacity, dtype=jnp.int32)
    send_table = (slot_iota[:, None] == slot_dest[None, :]).astype(jnp.bfloat16)
    take_table = (slot_dest[:, None] == slot_iota[None, :]).astype(jnp.float32)
    repeated = jnp.repeat(sent_rows, topk_count, axis=0)
    outgoing = jnp.dot(send_table, repeated, preferred_element_type=jnp.float32).astype(
        jnp.bfloat16
    )
    outgoing = outgoing.reshape(expert_count, capacity, -1)
    received = lax.all_to_all(outgoing, "grp", split_axis=0, concat_axis=0, tiled=True)
    item_lead = received.shape[0]
    item_count = received.shape[1]
    flat_rows = received.reshape(item_lead * item_count, -1)
    projected = jnp.dot(flat_rows, w_gate_up[0], preferred_element_type=jnp.float32)
    pairs_view = projected.reshape(item_lead * item_count, -1, 2)
    gate_half = pairs_view[..., 0]
    up_half = pairs_view[..., 1]
    activated = ((up_half + 1.0) * gate_half * jax.nn.sigmoid(swish_alpha * gate_half)).astype(
        jnp.bfloat16
    )
    down_part = jnp.dot(activated, w_down[0], preferred_element_type=jnp.float32).reshape(
        item_lead, item_count, -1
    )
    back_rows = lax.all_to_all(
        down_part.astype(jnp.bfloat16), "grp", split_axis=0, concat_axis=0, tiled=True
    ).astype(down_part.dtype)
    gathered = jnp.dot(
        take_table, back_rows.reshape(expert_count * capacity, -1), precision=lax.Precision.HIGHEST
    )
    weight_vec = route_weights.reshape(-1).astype(jnp.float32) / 65536.0
    mixture = jnp.sum((gathered * weight_vec[:, None]).reshape(row_count, topk_count, -1), axis=1)
    mixture = lax.psum_scatter(
        mixture.astype(jnp.bfloat16), "head", scatter_dimension=1, tiled=True
    ).astype(jnp.float32)
    return (hidden_here.astype(jnp.float32) + mixture).astype(jnp.bfloat16)


def solution(mesh):
    in_specs = (
        P("grp", None),
        P("grp", "head", None),
        P("grp", "head", None, None),
        P("grp", "head", None),
        P("grp"),
        P("head", None),
        P("head", None, None),
        P(),
        P("grp", None),
        P("grp", None),
        P("grp", None, "head"),
        P("grp", "head", None),
    )
    out_specs = P("grp", "head")
    return jax.shard_map(local, mesh=mesh, in_specs=in_specs, out_specs=out_specs, check_vma=False)
```

profile of v0, /device:TPU:0, one launch (start us, length us, event | category | flops | bytes accessed | tf_op | source)
XLA Modules:
  0.0 117.3 jit_solution(13345102271780202954)
XLA Ops:
  6.5 0.7 and_select_fusion
  7.2 0.7 fusion.25
  8.0 3.0 %copy.32 = bf16[16,4,128,128]{2,3,1,0:T(8,128)(2,1)S(1)} copy(bf16[16,4,128,128]{3,2,1,0:T(8,128)(2,1)} %param.14) | data formatting | bytes 4194304 | tf_op args[2]
  11.1 0.9 reshape.147
  12.0 1.2 %broadcast_select_fusion = bf16[16,4,128,128]{2,3,1,0:T(8,128)(2,1)S(1)} fusion(bf16[16,4,128,128]{2,3,1,0:T(8,128)(2,1)S(1)} %copy.32, pred[16,128]{1,0:T(8,128)(4,1)S(1)} %iota_compare_fusion.5, bf16[16,4,128]{2,1,0:T(4,128)(2,1)S(1)} %copy-done.1), kind=kLoop, calls=%fused_computation.8 | loop fusion | flops 1048576 | bytes 4212736 | tf_op jit(solution)/shard_map/jit(_where)/select_n | solution.py:27
  13.2 0.5 fusion.30
  13.7 0.3 fusion.17
  14.1 0.7 convolution_convert_fusion.2
  14.9 8.5 %copy.33 = bf16[4,256,2880]{2,1,0:T(8,128)(2,1)} copy(bf16[4,256,2880]{1,2,0:T(8,128)(2,1)} %param.18) | data formatting | bytes 11796480 | tf_op args[6]
  23.4 4.3 %convolution_convert_fusion.1 = bf16[16,2880]{1,0:T(8,128)(2,1)} fusion(bf16[16,1024]{1,0:T(8,128)(2,1)S(1)} %reshape.148, bf16[1024,2880]{1,0:T(8,128)(2,1)} %bitcast.29), kind=kOutput, calls=%fused_computation.7 | convolution fusion | flops 94417920 | bytes 6023168 | tf_op jit(solution)/shard_map/dot_general | solution.py:65
  27.9 0.2 convert_reduce_fusion
  28.1 20.3 %all-reduce.2.cloned.1.call-done = bf16[16,2880]{1,0:T(8,128)(2,1)} async-done(((bf16[16,2880]{1,0:T(8,128)(2,1)}), bf16[16,2880]{1,0:T(8,128)(2,1)}) %all-reduce.2.cloned.1.call-update) | async-done | bytes 92176 | tf_op jit(solution)/shard_map/psum | solution.py:68
  48.3 1.0 fusion.14
  49.6 0.2 reshape.151
  49.8 0.2 convolution_convert_fusion
  50.0 0.9 reshape.152
  50.9 6.8 %all-to-all-start = ((bf16[16,4,2880]{2,1,0:T(4,128)(2,1)}), bf16[16,4,2880]{2,1,0:T(4,128)(2,1)S(1)}, u32[]{:S(2)}, u32[]{:S(2)}) async-start(bf16[16,4,2880]{2,1,0:T(4,128)(2,1)} %reshape.152), calls=%async_computation | async-start | bytes 753664 | tf_op jit(solution)/shard_map/all_to_all | solution.py:90
  57.7 13.0 %dot_general.30 = bf16[720,2,2880]{2,1,0:T(2,128)(2,1)} reshape(bf16[1440,2880]{1,0:T(8,128)(2,1)} %bitcast.30) | data formatting | bytes 16588800 | tf_op jit(solution)/shard_map/dot_general | solution.py:94
  70.7 0.2 reshape.156
  70.9 6.0 %fusion = f32[64,720,2]{1,0,2:T(8,128)S(1)} fusion(bf16[64,2880,1]{1,0,2:T(8,128)(2,1)S(1)} %reshape.156, bf16[720,2,2880]{2,1,0:T(2,128)(2,1)} %dot_general.30), kind=kOutput, calls=%fused_computation | convolution fusion | flops 530841600 | bytes 9031680 | tf_op jit(solution)/shard_map/dot_general | solution.py:94
  77.0 3.0 %fusion.4 = bf16[16,4,2880]{2,0,1:T(8,128)(2,1)S(1)} fusion(bf16[1,720,2880]{2,1,0:T(8,128)(2,1)} %param.23, bf16[16,4,720]{2,1,0:T(4,128)(2,1)S(1)} %convert_element_type.75), kind=kOutput, calls=%fused_computation.5 | convolution fusion | flops 265605120 | bytes 4608000 | tf_op jit(solution)/shard_map/dot_general | solution.py:101
  80.0 0.9 copy.37
  80.9 6.9 %all-to-all-start.1 = ((bf16[16,4,2880]{2,1,0:T(4,128)(2,1)}), bf16[16,4,2880]{2,1,0:T(4,128)(2,1)S(1)}, u32[]{:S(2)}, u32[]{:S(2)}) async-start(bf16[16,4,2880]{2,1,0:T(4,128)(2,1)} %copy.37), calls=%async_computation.1 | async-start | bytes 753664 | tf_op jit(solution)/shard_map/all_to_all | solution.py:104
  88.0 12.0 %all-to-all-done.1 = bf16[16,4,2880]{2,1,0:T(4,128)(2,1)S(1)} async-done(((bf16[16,4,2880]{2,1,0:T(4,128)(2,1)}), bf16[16,4,2880]{2,1,0:T(4,128)(2,1)S(1)}, u32[]{:S(2)}, u32[]{:S(2)}) %all-to-all-start.1) | async-done | bytes 368672 | tf_op jit(solution)/shard_map/all_to_all | solution.py:104
  100.0 0.2 reshape.154
  100.2 0.3 convolution_multiply_fusion
  100.5 0.2 reshape.155
  100.7 0.5 reduce_sum.39
  101.2 1.2 copy.39
  102.4 6.3 %reduce-scatter.4.cloned.1.call-done = bf16[1440,16]{1,0:T(8,128)(2,1)} async-done(((bf16[2880,16]{1,0:T(8,128)(2,1)}), bf16[1440,16]{1,0:T(8,128)(2,1)}) %reduce-scatter.4.cloned.1.call-update) | async-done | bytes 46096
  108.7 1.1 copy.40
  109.8 0.7 add_convert_fusion.1
  (34 shorter events, 1.0 us)
Async XLA Ops:
  6.5 5.4 %copy-start.1 = (bf16[16,4,128]{2,1,0:T(4,128)(2,1)S(1)}, bf16[16,4,128]{2,1,0:T(4,128)(2,1)}, u32[]{:S(2)}) copy-start(bf16[16,4,128]{2,1,0:T(4,128)(2,1)} %param.15) | copy-start | bytes 49156
  6.5 41.8 %all-reduce.2.cloned.1.call-start = ((), (), s32[]{:S(2)}) async-start(), calls=%async_computation.3 | async-start | bytes 188416 | tf_op jit(solution)/shard_map/psum | solution.py:68
  8.0 5.8 %copy-start.3 = (f32[4,4]{1,0:T(4,128)S(1)}, f32[4,4]{1,0:T(4,128)}, u32[]{:S(2)}) copy-start(f32[4,4]{1,0:T(4,128)} %param.17) | copy-start | bytes 196
  23.4 4.3 %copy-start.4 = (s32[16,4]{0,1:T(4,128)S(1)}, s32[16,4]{0,1:T(4,128)}, u32[]{:S(2)}) copy-start(s32[16,4]{0,1:T(4,128)} %param.20) | copy-start | bytes 772
  23.4 25.0 %copy-start = (bf16[16,2880]{1,0:T(8,128)(2,1)S(1)}, bf16[16,2880]{1,0:T(8,128)(2,1)}, u32[]{:S(2)}) copy-start(bf16[16,2880]{1,0:T(8,128)(2,1)} %param.12) | copy-start | bytes 276484
  23.4 26.0 %copy-start.2 = (f32[2880]{0:T(1024)S(1)}, f32[2880]{0:T(1024)}, u32[]{:S(2)}) copy-start(f32[2880]{0:T(1024)} %param.19) | copy-start | bytes 34564
  50.9 19.8 %all-to-all-start = ((bf16[16,4,2880]{2,1,0:T(4,128)(2,1)}), bf16[16,4,2880]{2,1,0:T(4,128)(2,1)S(1)}, u32[]{:S(2)}, u32[]{:S(2)}) async-start(bf16[16,4,2880]{2,1,0:T(4,128)(2,1)} %reshape.152), calls=%async_computation | async-start | bytes 753664 | tf_op jit(solution)/shard_map/all_to_all | solution.py:90
  76.9 11.0 %copy-start.5 = (s32[16,4]{0,1:T(4,128)S(1)}, s32[16,4]{0,1:T(4,128)}, u32[]{:S(2)}) copy-start(s32[16,4]{0,1:T(4,128)} %param.21) | copy-start | bytes 772
  80.9 19.1 %all-to-all-start.1 = ((bf16[16,4,2880]{2,1,0:T(4,128)(2,1)}), bf16[16,4,2880]{2,1,0:T(4,128)(2,1)S(1)}, u32[]{:S(2)}, u32[]{:S(2)}) async-start(bf16[16,4,2880]{2,1,0:T(4,128)(2,1)} %copy.37), calls=%async_computation.1 | async-start | bytes 753664 | tf_op jit(solution)/shard_map/all_to_all | solution.py:104
  87.8 20.9 %reduce-scatter.4.cloned.1.call-start = ((), (), s32[]{:S(2)}) async-start(), calls=%async_computation.4 | async-start | bytes 1105920
Sparse Core Ops, SparseCore 0:
  27.8 20.4 all-reduce.1
  102.5 6.1 reduce-scatter.3
where the time goes:
time: 118 us; the launch traced here: 117 us
  waiting for transfers between devices  38.6 us (33%)
  local copies, waits for them, and re-layouts  30.7 us (26%)
  matrix products  15 us (13%)
  starting transfers between devices  13.8 us (12%)
  between operations  13.6 us (12%)
  other arithmetic  5.62 us (5%)
    psum x1, waiting for transfers between devices, local(): lax.psum(partial_value.astype(jnp.bfloat16), 'head').astype(jnp.float32)  20.3 us
    unnamed x19, local copies, waits for them, and re-layouts  13.9 us
    dot_general x1, local copies, waits for them, and re-layouts, local(): jnp.dot(flat_rows, w_gate_up[0], preferred_element_type=jnp.float32)  13 us
    all_to_all x1, waiting for transfers between devices, local(): lax.all_to_all(down_part.astype(jnp.bfloat16), 'grp', split_axis=0, conca...  12 us
    all_to_all x1, starting transfers between devices, local(): lax.all_to_all(down_part.astype(jnp.bfloat16), 'grp', split_axis=0, conca...  6.91 us
    all_to_all x1, starting transfers between devices, local(): lax.all_to_all(outgoing, 'grp', split_axis=0, concat_axis=0, tiled=True)  6.82 us
    unnamed x3, waiting for transfers between devices  6.31 us
    dot_general x1, matrix products, local(): jnp.dot(flat_rows, w_gate_up[0], preferred_element_type=jnp.float32)  5.99 us
  transfers between devices with their start and end apart: 4, of which 3 were waited for; matrix products, arithmetic and copies ran while one was open for 11% of the time, Pallas kernels for 0%

commit v1 on v0

--- a/solution.py
+++ b/solution.py
@@ -1,6 +1,10 @@
+import functools
+
 import jax
 import jax.numpy as jnp
 from jax import lax
+from jax.experimental import pallas as pl
+from jax.experimental.pallas import tpu as pltpu
 from jax.sharding import PartitionSpec as P
 
 epsilon = 1e-05
@@ -115,6 +119,450 @@
     return (hidden_here.astype(jnp.float32) + mixture).astype(jnp.bfloat16)
 
 
+MESH = pl.DeviceIdType.MESH
+NT = (((1,), (1,)), ((), ()))
+
+
+def fused_fits(mesh, args):
+    queries, kv_cache = args[1], args[2]
+    grp, head = mesh.shape["grp"], mesh.shape["head"]
+    rows, heads, width = queries.shape
+    half = kv_cache.shape[3] // 2
+    return (
+        head == 2
+        and grp % 4 == 0
+        and kv_cache.shape[3] == 128
+        and kv_cache.shape[2] % 128 == 0
+        and (width // half) % 2 == 0
+        and rows % 16 == 0
+        and heads * (width // half) % 16 == 0
+        and capacity_of(rows, args[8].shape[1], grp) == 4
+    )
+
+
+def capacity_of(rows, topk, experts):
+    return max(2, rows * topk // experts)
+
+
+def largest_part(count, limit):
+    return max(size for size in range(16, limit + 1, 16) if count % size == 0)
+
+
+def fused_kernel(
+    n,
+    residual,
+    queries,
+    new_kv,
+    positions,
+    sinks,
+    gain,
+    ids,
+    route_w,
+    kv_hbm,
+    wo_hbm,
+    wgu_hbm,
+    wd_hbm,
+    out,
+    kv,
+    wo,
+    wgu,
+    wd,
+    q2,
+    nv,
+    mix,
+    part_tx,
+    part_rx,
+    tx,
+    rx,
+    flat,
+    x_in,
+    proj,
+    act,
+    ex_tx,
+    ex_rx,
+    back_tx,
+    back_rx,
+    back_flat,
+    local_sem,
+    part_sem,
+    disp_send,
+    disp_recv,
+    fwd_send,
+    ex_send,
+    ex_recv,
+    back_send,
+    back_recv,
+):
+    rows, width = residual.shape
+    half = out.shape[1]
+    heads = queries.shape[1]
+    win, kv_width = kv.shape[2], kv.shape[3]
+    hd = kv_width // 2
+    groups = queries.shape[2] // hd
+    qrows = heads * groups
+    topk = ids.shape[0]
+    cap = tx.shape[1]
+    slots = n * cap
+    hidden_units = wd.shape[0]
+    f32, bf16 = jnp.float32, jnp.bfloat16
+
+    b = lax.axis_index("grp")
+    h = lax.axis_index("head")
+    partner = 1 - h
+
+    loads = [
+        pltpu.make_async_copy(src, dst, local_sem.at[i])
+        for i, (src, dst) in enumerate(
+            ((kv_hbm, kv), (wo_hbm, wo), (wgu_hbm, wgu), (wd_hbm, wd))
+        )
+    ]
+    for load in loads:
+        load.start()
+
+    barrier = pltpu.get_barrier_semaphore()
+    pl.semaphore_signal(barrier, inc=1, device_id=(b, partner), device_id_type=MESH)
+
+    def greet(d, carry):
+        pl.semaphore_signal(
+            barrier, inc=1, device_id=(lax.rem(b + d, n), h), device_id_type=MESH
+        )
+        return carry
+
+    lax.fori_loop(1, n, greet, 0)
+
+    lane = lax.broadcasted_iota(jnp.int32, (rows, heads, kv_width), 2)
+    fresh = new_kv[...].astype(f32)
+    for g in range(groups):
+        at = g // 2 * kv_width
+        piece = queries[:, :, at : at + kv_width].astype(f32)
+        if g % 2:
+            piece = pltpu.roll(piece, hd, 2)
+        q2[:, g * heads : (g + 1) * heads, :] = jnp.where(lane < hd, piece, 0.0)
+        nv[:, g * heads : (g + 1) * heads, :] = fresh
+
+    row_iota = lax.broadcasted_iota(jnp.int32, (qrows, 1), 0)
+    sink = jnp.zeros((qrows, 1), f32)
+    for g in range(groups):
+        for k in range(heads):
+            sink = jnp.where(row_iota == g * heads + k, sinks[k, g], sink)
+    r_iota = lax.broadcasted_iota(jnp.int32, (qrows, heads * win), 0)
+    c_iota = lax.broadcasted_iota(jnp.int32, (qrows, heads * win), 1)
+    own_block = lax.rem(r_iota, heads) == c_iota // win
+    slot = lax.rem(c_iota, win)
+    scale = hd ** (-0.5)
+
+    loads[0].wait()
+
+    def attend_one(t, carry):
+        p = positions[t]
+        cur = lax.rem(p, win)
+        q = q2[t]
+        new = nv[t]
+        cache = kv[t].reshape(heads * win, kv_width)
+        s = lax.dot_general(q.astype(bf16), cache, NT, preferred_element_type=f32) * scale
+        s_new = jnp.sum(q * new, axis=1, keepdims=True) * scale
+        is_new = slot == cur
+        s = jnp.where(is_new, s_new, s)
+        lag = cur - slot
+        lag = jnp.where(lag < 0, lag + win, lag)
+        s = jnp.where(own_block & (lag <= p), s, -jnp.inf)
+        m = jnp.maximum(jnp.max(s, axis=1, keepdims=True), sink)
+        e = jnp.exp(s - m)
+        inv = 1.0 / (jnp.sum(e, axis=1, keepdims=True) + jnp.exp(sink - m))
+        w = e * inv
+        w_old = jnp.where(is_new, 0.0, w).astype(bf16)
+        w_new = jnp.sum(jnp.where(is_new, w, 0.0), axis=1, keepdims=True).astype(bf16).astype(f32)
+        o = jnp.dot(w_old, cache, preferred_element_type=f32) + w_new * new
+        mix[pl.ds(pl.multiple_of(t * qrows, qrows), qrows), :] = o
+        return carry
+
+    lax.fori_loop(0, rows, attend_one, 0, unroll=4)
+
+    lane2 = lax.broadcasted_iota(jnp.int32, (rows, kv_width), 1)
+    loads[1].wait()
+    acc = jnp.zeros((rows, width), f32)
+    for k in range(heads):
+        pairs = []
+        for g in range(0, groups, 2):
+            even = mix[pl.ds(g * heads + k, rows, stride=qrows), :]
+            odd = mix[pl.ds((g + 1) * heads + k, rows, stride=qrows), :]
+            pairs.append(jnp.where(lane2 < hd, pltpu.roll(even, hd, 1), odd))
+        mixed = jnp.concatenate(pairs, axis=1).astype(bf16)
+        acc += lax.dot_general(mixed, wo[k], NT, preferred_element_type=f32)
+    part_tx[...] = acc.astype(bf16)
+
+    pl.semaphore_wait(barrier, n)
+    part = pltpu.make_async_remote_copy(
+        src_ref=part_tx,
+        dst_ref=part_rx,
+        send_sem=part_sem.at[0],
+        recv_sem=part_sem.at[1],
+        device_id=(b, partner),
+        device_id_type=MESH,
+    )
+    part.start()
+
+    t_row = lax.broadcasted_iota(jnp.int32, (slots, rows), 0)
+    rel, slot_c = t_row // cap, lax.rem(t_row, cap)
+    named = jnp.zeros((slots, rows), jnp.int32)
+    weight = jnp.zeros((slots, rows), jnp.int32)
+    for k in range(topk):
+        other = ids[k : k + 1, :] - b
+        other = jnp.where(other < 0, other + n, other)
+        hit = rel == other
+        named = jnp.where(hit, 1, named)
+        weight = jnp.where(hit, route_w[k : k + 1, :], weight)
+    before = (
+        lax.broadcasted_iota(jnp.int32, (rows, rows), 0)
+        < lax.broadcasted_iota(jnp.int32, (rows, rows), 1)
+    )
+    rank = jnp.dot(
+        named.astype(f32).astype(bf16),
+        before.astype(f32).astype(bf16),
+        preferred_element_type=f32,
+    )
+    chosen = (named > 0) & (rank == slot_c.astype(f32))
+    table = chosen.astype(f32).astype(bf16)
+    weight = jnp.where(chosen, weight, 0)
+    high = weight // 256
+    low = weight - high * 256
+    eye = (
+        lax.broadcasted_iota(jnp.int32, (rows, rows), 0)
+        == lax.broadcasted_iota(jnp.int32, (rows, rows), 1)
+    )
+    eye = eye.astype(f32).astype(bf16)
+    comb_high = lax.dot_general(
+        eye, high.astype(f32).astype(bf16), NT, preferred_element_type=f32
+    ).astype(bf16)
+    comb_low = lax.dot_general(
+        eye, low.astype(f32).astype(bf16), NT, preferred_element_type=f32
+    ).astype(bf16)
+
+    part.wait()
+    attention = part_tx[...].astype(f32) + part_rx[...].astype(f32)
+    hidden = (residual[...].astype(f32) + attention).astype(bf16).astype(f32)
+    mean_square = jnp.sum(hidden * hidden, axis=1, keepdims=True) * (1.0 / width)
+    normed = (hidden * lax.rsqrt(mean_square + epsilon) * gain[...]).astype(bf16)
+    outgoing = jnp.dot(table, normed, preferred_element_type=f32)
+    flat[0:cap, :] = outgoing[0:cap]
+    for d in range(1, n):
+        tx[d] = outgoing[d * cap : (d + 1) * cap].astype(bf16)
+
+    def disp(d):
+        return pltpu.make_async_remote_copy(
+            src_ref=tx.at[d],
+            dst_ref=rx.at[d],
+            send_sem=disp_send.at[d],
+            recv_sem=disp_recv.at[d],
+            device_id=(lax.rem(b + d, n), h),
+            device_id_type=MESH,
+        )
+
+    def fwd(d):
+        return pltpu.make_async_remote_copy(
+            src_ref=rx.at[d],
+            dst_ref=rx.at[d],
+            send_sem=fwd_send.at[d],
+            recv_sem=disp_recv.at[d],
+            device_id=(b, partner),
+            device_id_type=MESH,
+        )
+
+    def each(offset, action):
+        def step(j, carry):
+            d = 2 * j + offset
+
+            @pl.when(d > 0)
+            def _():
+                action(d)
+
+            return carry
+
+        lax.fori_loop(0, n // 2, step, 0)
+
+    def pass_on(d):
+        disp(d).wait_recv()
+        fwd(d).start()
+
+    each(h, lambda d: disp(d).start())
+    each(h, pass_on)
+    each(partner, lambda d: fwd(d).wait_recv())
+
+    for d in range(1, n):
+        flat[d * cap : (d + 1) * cap, :] = rx[d].astype(f32)
+    x_in[...] = flat[...].astype(bf16)
+
+    loads[2].wait()
+    step_rows = largest_part(wgu.shape[0], 256)
+
+    def gate_up(i, carry):
+        at = pl.ds(pl.multiple_of(i * step_rows, step_rows), step_rows)
+        proj[at, 0:slots] = lax.dot_general(
+            wgu[at, :], x_in[...], NT, preferred_element_type=f32
+        )
+        return carry
+
+    lax.fori_loop(0, wgu.shape[0] // step_rows, gate_up, 0)
+
+    gate = proj[pl.ds(0, hidden_units, stride=2), :]
+    up = proj[pl.ds(1, hidden_units, stride=2), :]
+    act[0:hidden_units, :] = (up + 1.0) * gate * (1.0 / (1.0 + jnp.exp(-swish_alpha * gate)))
+    if act.shape[0] > hidden_units:
+        act[hidden_units:, :] = jnp.zeros((act.shape[0] - hidden_units, act.shape[1]), f32)
+    activated = act[...].T[0:slots, 0:hidden_units].astype(bf16)
+
+    loads[3].wait()
+    down = jnp.dot(activated, wd[...], preferred_element_type=f32)
+    left, right = down[:, 0:half], down[:, half:width]
+    mine = jnp.where(h == 0, left, right)
+    ex_tx[...] = jnp.where(h == 0, right, left).astype(bf16)
+
+    def exchange(i):
+        at = pl.ds(i * 16, 16)
+        return pltpu.make_async_remote_copy(
+            src_ref=ex_tx.at[at, :],
+            dst_ref=ex_rx.at[at, :],
+            send_sem=ex_send.at[i],
+            recv_sem=ex_recv.at[i],
+            device_id=(b, partner),
+            device_id_type=MESH,
+        )
+
+    def give_back(d):
+        return pltpu.make_async_remote_copy(
+            src_ref=back_tx.at[d],
+            dst_ref=back_rx.at[d],
+            send_sem=back_send.at[d],
+            recv_sem=back_recv.at[d],
+            device_id=(lax.rem(b + n - d, n), h),
+            device_id_type=MESH,
+        )
+
+    parts = slots // 16
+    per_part = 16 // cap
+    for i in range(parts):
+        exchange(i).start()
+    for i in range(parts):
+        exchange(i).wait_recv()
+        total = mine[i * 16 : (i + 1) * 16] + ex_rx[i * 16 : (i + 1) * 16, :].astype(f32)
+        for j in range(per_part):
+            d = i * per_part + j
+            block = total[j * cap : (j + 1) * cap]
+            if d == 0:
+                back_flat[0:cap, :] = block
+            else:
+                back_tx[d] = block.astype(bf16)
+                give_back(d).start()
+
+    hidden_here = jnp.where(h == 0, hidden[:, 0:half], hidden[:, half:width])
+
+    for d in range(1, n):
+        give_back(d).wait_recv()
+        back_flat[d * cap : (d + 1) * cap, :] = back_rx[d].astype(f32)
+    rows_back = back_flat[...].astype(bf16)
+    mixture = jnp.dot(comb_high, rows_back, preferred_element_type=f32) * (1.0 / 256)
+    mixture += jnp.dot(comb_low, rows_back, preferred_element_type=f32) * (1.0 / 65536)
+    out[...] = (hidden_here + mixture).astype(bf16)
+
+    each(h, lambda d: disp(d).wait_send())
+    each(h, lambda d: fwd(d).wait_send())
+    for i in range(parts):
+        exchange(i).wait_send()
+
+    def sent(d, carry):
+        give_back(d).wait_send()
+        return carry
+
+    lax.fori_loop(1, n, sent, 0)
+
+
+def fused(
+    n,
+    residual,
+    queries,
+    kv_cache,
+    new_kv,
+    positions,
+    sink_logits,
+    out_proj,
+    norm_gain,
+    route_ids,
+    route_weights,
+    w_gate_up,
+    w_down,
+):
+    rows, width = residual.shape
+    half = width // 2
+    heads = queries.shape[1]
+    kv_width = kv_cache.shape[3]
+    groups = queries.shape[2] * 2 // kv_width
+    cap = capacity_of(rows, route_ids.shape[1], n)
+    slots = n * cap
+    lanes = -(-slots // 128) * 128
+    units = w_down.shape[1]
+    f32, bf16 = jnp.float32, jnp.bfloat16
+    vmem = pl.BlockSpec(memory_space=pltpu.VMEM)
+    smem = pl.BlockSpec(memory_space=pltpu.SMEM)
+    hbm = pl.BlockSpec(memory_space=pl.ANY)
+    dma = pltpu.SemaphoreType.DMA
+    wo = jnp.swapaxes(out_proj, 1, 2)
+    wgu = jnp.swapaxes(w_gate_up[0], 0, 1)
+    wd = w_down[0]
+    return pl.pallas_call(
+        functools.partial(fused_kernel, n),
+        out_shape=jax.ShapeDtypeStruct((rows, half), bf16),
+        in_specs=[vmem, vmem, vmem, smem, smem, vmem, vmem, vmem, hbm, hbm, hbm, hbm],
+        out_specs=vmem,
+        scratch_shapes=[
+            pltpu.VMEM(kv_cache.shape, bf16),
+            pltpu.VMEM(wo.shape, bf16),
+            pltpu.VMEM(wgu.shape, bf16),
+            pltpu.VMEM(wd.shape, bf16),
+            pltpu.VMEM((rows, heads * groups, kv_width), f32),
+            pltpu.VMEM((rows, heads * groups, kv_width), f32),
+            pltpu.VMEM((rows * heads * groups, kv_width), f32),
+            pltpu.VMEM((rows, width), bf16),
+            pltpu.VMEM((rows, width), bf16),
+            pltpu.VMEM((n, cap, width), bf16),
+            pltpu.VMEM((n, cap, width), bf16),
+            pltpu.VMEM((slots, width), f32),
+            pltpu.VMEM((slots, width), bf16),
+            pltpu.VMEM((2 * units, lanes), f32),
+            pltpu.VMEM((-(-units // 128) * 128, lanes), f32),
+            pltpu.VMEM((slots, half), bf16),
+            pltpu.VMEM((slots, half), bf16),
+            pltpu.VMEM((n, cap, half), bf16),
+            pltpu.VMEM((n, cap, half), bf16),
+            pltpu.VMEM((slots, half), f32),
+            dma((4,)),
+            dma((2,)),
+            dma((n,)),
+            dma((n,)),
+            dma((n,)),
+            dma((slots // 16,)),
+            dma((slots // 16,)),
+            dma((n,)),
+            dma((n,)),
+        ],
+        compiler_params=pltpu.CompilerParams(
+            collective_id=0, has_side_effects=True, vmem_limit_bytes=48 * 1024 * 1024
+        ),
+    )(
+        residual,
+        queries,
+        new_kv,
+        positions,
+        sink_logits,
+        norm_gain.reshape(1, width),
+        route_ids.T,
+        route_weights.T,
+        kv_cache,
+        wo,
+        wgu,
+        wd,
+    )
+
+
 def solution(mesh):
     in_specs = (
         P("grp", None),
@@ -131,4 +579,9 @@
         P("grp", "head", None),
     )
     out_specs = P("grp", "head")
-    return jax.shard_map(local, mesh=mesh, in_specs=in_specs, out_specs=out_specs, check_vma=False)
+    def body(*args):
+        if fused_fits(mesh, args):
+            return fused(mesh.shape["grp"], *args)
+        return local(*args)
+
+    return jax.shard_map(body, mesh=mesh, in_specs=in_specs, out_specs=out_specs, check_vma=False)

time: 118 us -> 42.5 us (0.36)
  waiting for transfers between devices: 38.6 us -> 0 us
  Pallas kernels: 0 us -> 34.1 us
  local copies, waits for them, and re-layouts: 30.7 us -> 7.99 us
  matrix products: 15 us -> 0 us
  starting transfers between devices: 13.8 us -> 0 us
  between operations: 13.6 us -> 0.02 us
  other arithmetic: 5.62 us -> 0 us
    pallas_call x0 -> x1, Pallas kernels: none -> 34.1 us  [fused(): pl.pallas_call(functools.partial(fused_kernel, n), out_shape=jax.ShapeDty...]
    psum x1 -> x0, waiting for transfers between devices: 20.3 us -> none  [local(): lax.psum(partial_value.astype(jnp.bfloat16), 'head').astype(jnp.float32)]
    dot_general x7 -> x0, matrix products: 15 us -> none  [the longest x1 5.99 us: local(): jnp.dot(flat_rows, w_gate_up[0], preferred_element_type=jnp.float32)]
    all_to_all x2 -> x0, starting transfers between devices: 13.7 us -> none  [the longest x1 6.91 us: local(): lax.all_to_all(down_part.astype(jnp.bfloat16), 'grp', split_axis=0, conca...]
    dot_general x1 -> x0, local copies, waits for them, and re-layouts: 13 us -> none  [local(): jnp.dot(flat_rows, w_gate_up[0], preferred_element_type=jnp.float32)]
    all_to_all x2 -> x0, waiting for transfers between devices: 12 us -> none  [the longest x1 12 us: local(): lax.all_to_all(down_part.astype(jnp.bfloat16), 'grp', split_axis=0, conca...]
    unnamed x19 -> x17, local copies, waits for them, and re-layouts: 13.9 us -> 7.27 us
    unnamed x3 -> x0, waiting for transfers between devices: 6.31 us -> none
  transfers between devices with their start and end apart: 4 -> 0, of which waited for: 3 -> 0; matrix products, arithmetic and copies ran while one was open for 11% -> 0% of each run, Pallas kernels for 0% -> 0%
where the time goes in v1:
time: 42.5 us; the launch traced here: 42.1 us
  Pallas kernels  34.1 us (80%)
  local copies, waits for them, and re-layouts  7.99 us (19%)
    pallas_call x1, Pallas kernels, fused(): pl.pallas_call(functools.partial(fused_kernel, n), out_shape=jax.ShapeDty...  34.1 us
    unnamed x17, local copies, waits for them, and re-layouts  7.27 us

profile of v1, /device:TPU:0, one launch (start us, length us, event | category | flops | bytes accessed | tf_op | source)
XLA Modules:
  0.0 42.1 jit_solution(10216978800957385234)
XLA Ops:
  0.0 0.7 %reshape.3.gain = f32[1,2880]{1,0:T(1,128)S(1)} reshape(f32[2880]{0:T(1024)} %param.19) | data formatting | bytes 23040 | tf_op jit(solution)/shard_map/reshape | solution.py:556
  0.7 0.0 copy-start
  0.7 1.6 %copy-done = bf16[16,4,128,128]{3,2,1,0:T(8,128)(2,1)S(1)} copy-done((bf16[16,4,128,128]{3,2,1,0:T(8,128)(2,1)S(1)}, bf16[16,4,128,128]{3,2,1,0:T(8,128)(2,1)}, u32[]{:S(2)}) %copy-start) | copy-done | bytes 2097176
  2.3 0.0 copy-start.1
  2.3 0.9 %copy-done.1 = bf16[16,2880]{1,0:T(8,128)(2,1)S(1)} copy-done((bf16[16,2880]{1,0:T(8,128)(2,1)S(1)}, bf16[16,2880]{1,0:T(8,128)(2,1)}, u32[]{:S(2)}) %copy-start.1) | copy-done | bytes 92184
  3.2 0.0 copy-start.2
  3.2 0.8 %copy-done.2 = bf16[16,4,256]{2,1,0:T(4,128)(2,1)S(1)} copy-done((bf16[16,4,256]{2,1,0:T(4,128)(2,1)S(1)}, bf16[16,4,256]{2,1,0:T(4,128)(2,1)}, u32[]{:S(2)}) %copy-start.2) | copy-done | bytes 32792
  4.0 0.0 copy-start.3
  4.0 0.7 %copy-done.3 = bf16[16,4,128]{2,1,0:T(4,128)(2,1)S(1)} copy-done((bf16[16,4,128]{2,1,0:T(4,128)(2,1)S(1)}, bf16[16,4,128]{2,1,0:T(4,128)(2,1)}, u32[]{:S(2)}) %copy-start.3) | copy-done | bytes 16408
  4.7 0.0 copy-start.4
  4.7 0.7 %copy-done.4 = f32[4,4]{1,0:T(4,128)S(1)} copy-done((f32[4,4]{1,0:T(4,128)S(1)}, f32[4,4]{1,0:T(4,128)}, u32[]{:S(2)}) %copy-start.4) | copy-done | bytes 88
  5.4 0.0 copy-start.5
  5.4 0.7 %copy-done.5 = s32[16,4]{0,1:T(4,128)S(1)} copy-done((s32[16,4]{0,1:T(4,128)S(1)}, s32[16,4]{0,1:T(4,128)}, u32[]{:S(2)}) %copy-start.5) | copy-done | bytes 280
  6.0 0.0 copy-start.6
  6.0 0.7 %copy-done.6 = s32[16,4]{0,1:T(4,128)S(1)} copy-done((s32[16,4]{0,1:T(4,128)S(1)}, s32[16,4]{0,1:T(4,128)}, u32[]{:S(2)}) %copy-start.6) | copy-done | bytes 280
  6.7 0.0 copy-start.7
  6.7 0.7 %copy-done.7 = s32[16]{0:T(128)S(1)} copy-done((s32[16]{0:T(128)S(1)}, s32[16]{0:T(128)}, u32[]{:S(2)}) %copy-start.7) | copy-done | bytes 88
  7.4 34.1 %shard_map.118 = bf16[16,1440]{1,0:T(8,128)(2,1)S(1)} custom-call(bf16[16,2880]{1,0:T(8,128)(2,1)S(1)} %copy-done.1, bf16[16,4,256]{2,1,0:T(4,128)(2,1)S(1)} %copy-done.2, bf16[16,4,128]{2,1,0:T(4,128)(2,1)S(1)} %copy-done.3, s32[16]{0:T(128)S(1)} %copy-done.7, f32[4,4]{1,0:T(4,128)S(1)} %copy-done.4, f32[1,2880]{1,0:T(1,128)S(1)} %reshape.3.gain, ...), custom_call_target="tpu_custom_call" | custom-call | tf_op jit(solution)/shard_map/pallas_call | solution.py:511
  41.5 0.6 %copy.14 = bf16[16,1440]{1,0:T(8,128)(2,1)} copy(bf16[16,1440]{1,0:T(8,128)(2,1)S(1)} %shard_map.118) | data formatting | bytes 92160
Async XLA Ops:
  0.7 1.6 %copy-start = (bf16[16,4,128,128]{3,2,1,0:T(8,128)(2,1)S(1)}, bf16[16,4,128,128]{3,2,1,0:T(8,128)(2,1)}, u32[]{:S(2)}) copy-start(bf16[16,4,128,128]{3,2,1,0:T(8,128)(2,1)} %kv_hbm.1) | copy-start | bytes 6291460
  2.3 0.9 %copy-start.1 = (bf16[16,2880]{1,0:T(8,128)(2,1)S(1)}, bf16[16,2880]{1,0:T(8,128)(2,1)}, u32[]{:S(2)}) copy-start(bf16[16,2880]{1,0:T(8,128)(2,1)} %residual.1) | copy-start | bytes 276484
  3.2 0.8 %copy-start.2 = (bf16[16,4,256]{2,1,0:T(4,128)(2,1)S(1)}, bf16[16,4,256]{2,1,0:T(4,128)(2,1)}, u32[]{:S(2)}) copy-start(bf16[16,4,256]{2,1,0:T(4,128)(2,1)} %queries.1) | copy-start | bytes 98308
  4.0 0.7 %copy-start.3 = (bf16[16,4,128]{2,1,0:T(4,128)(2,1)S(1)}, bf16[16,4,128]{2,1,0:T(4,128)(2,1)}, u32[]{:S(2)}) copy-start(bf16[16,4,128]{2,1,0:T(4,128)(2,1)} %new_kv.1) | copy-start | bytes 49156
  4.7 0.7 %copy-start.4 = (f32[4,4]{1,0:T(4,128)S(1)}, f32[4,4]{1,0:T(4,128)}, u32[]{:S(2)}) copy-start(f32[4,4]{1,0:T(4,128)} %sinks.1) | copy-start | bytes 196
  5.4 0.7 %copy-start.5 = (s32[16,4]{0,1:T(4,128)S(1)}, s32[16,4]{0,1:T(4,128)}, u32[]{:S(2)}) copy-start(s32[16,4]{0,1:T(4,128)} %param.20) | copy-start | bytes 772
  6.0 0.7 %copy-start.6 = (s32[16,4]{0,1:T(4,128)S(1)}, s32[16,4]{0,1:T(4,128)}, u32[]{:S(2)}) copy-start(s32[16,4]{0,1:T(4,128)} %param.21) | copy-start | bytes 772
  6.7 0.7 %copy-start.7 = (s32[16]{0:T(128)S(1)}, s32[16]{0:T(128)}, u32[]{:S(2)}) copy-start(s32[16]{0:T(128)} %positions.1) | copy-start | bytes 196

commit v2 on v1

--- a/solution.py
+++ b/solution.py
@@ -150,19 +150,27 @@
 
 def fused_kernel(
     n,
-    residual,
-    queries,
-    new_kv,
-    positions,
-    sinks,
-    gain,
-    ids,
-    route_w,
+    positions_hbm,
+    sinks_hbm,
+    queries_hbm,
+    new_kv_hbm,
     kv_hbm,
     wo_hbm,
+    ids_hbm,
+    route_w_hbm,
+    residual_hbm,
+    gain_hbm,
     wgu_hbm,
     wd_hbm,
     out,
+    positions,
+    sinks,
+    queries,
+    new_kv,
+    ids,
+    route_w,
+    residual,
+    gain,
     kv,
     wo,
     wgu,
@@ -213,10 +221,23 @@
     loads = [
         pltpu.make_async_copy(src, dst, local_sem.at[i])
         for i, (src, dst) in enumerate(
-            ((kv_hbm, kv), (wo_hbm, wo), (wgu_hbm, wgu), (wd_hbm, wd))
+            (
+                (positions_hbm, positions),
+                (sinks_hbm, sinks),
+                (queries_hbm, queries),
+                (new_kv_hbm, new_kv),
+                (kv_hbm, kv),
+                (wo_hbm, wo),
+                (ids_hbm, ids),
+                (route_w_hbm, route_w),
+                (residual_hbm, residual),
+                (gain_hbm, gain),
+                (wgu_hbm, wgu),
+                (wd_hbm, wd),
+            )
         )
     ]
-    for load in loads:
+    for load in loads[0:10]:
         load.start()
 
     barrier = pltpu.get_barrier_semaphore()
@@ -229,6 +250,9 @@
         return carry
 
     lax.fori_loop(1, n, greet, 0)
+
+    for load in loads[0:4]:
+        load.wait()
 
     lane = lax.broadcasted_iota(jnp.int32, (rows, heads, kv_width), 2)
     fresh = new_kv[...].astype(f32)
@@ -251,7 +275,7 @@
     slot = lax.rem(c_iota, win)
     scale = hd ** (-0.5)
 
-    loads[0].wait()
+    loads[4].wait()
 
     def attend_one(t, carry):
         p = positions[t]
@@ -276,10 +300,12 @@
         mix[pl.ds(pl.multiple_of(t * qrows, qrows), qrows), :] = o
         return carry
 
-    lax.fori_loop(0, rows, attend_one, 0, unroll=4)
+    lax.fori_loop(0, rows, attend_one, 0, unroll=8)
 
     lane2 = lax.broadcasted_iota(jnp.int32, (rows, kv_width), 1)
-    loads[1].wait()
+    loads[5].wait()
+    for load in loads[10:]:
+        load.start()
     acc = jnp.zeros((rows, width), f32)
     for k in range(heads):
         pairs = []
@@ -301,6 +327,9 @@
         device_id_type=MESH,
     )
     part.start()
+
+    for load in loads[6:10]:
+        load.wait()
 
     t_row = lax.broadcasted_iota(jnp.int32, (slots, rows), 0)
     rel, slot_c = t_row // cap, lax.rem(t_row, cap)
@@ -342,7 +371,7 @@
     attention = part_tx[...].astype(f32) + part_rx[...].astype(f32)
     hidden = (residual[...].astype(f32) + attention).astype(bf16).astype(f32)
     mean_square = jnp.sum(hidden * hidden, axis=1, keepdims=True) * (1.0 / width)
-    normed = (hidden * lax.rsqrt(mean_square + epsilon) * gain[...]).astype(bf16)
+    normed = (hidden * lax.rsqrt(mean_square + epsilon) * gain[...].reshape(1, width)).astype(bf16)
     outgoing = jnp.dot(table, normed, preferred_element_type=f32)
     flat[0:cap, :] = outgoing[0:cap]
     for d in range(1, n):
@@ -368,9 +397,12 @@
             device_id_type=MESH,
         )
 
-    def each(offset, action):
+    def each(parity, action, near_first=False):
         def step(j, carry):
-            d = 2 * j + offset
+            j = n // 2 - 1 - j if near_first else j
+            even = (j + 1) // 2 * 2 * (1 - j % 2 * 2)
+            odd = (j // 2 * 2 + 1) * (j % 2 * 2 - 1)
+            d = n // 2 + parity * odd + (1 - parity) * even
 
             @pl.when(d > 0)
             def _():
@@ -385,15 +417,15 @@
         fwd(d).start()
 
     each(h, lambda d: disp(d).start())
-    each(h, pass_on)
-    each(partner, lambda d: fwd(d).wait_recv())
+    each(h, pass_on, near_first=True)
+    each(partner, lambda d: fwd(d).wait_recv(), near_first=True)
 
     for d in range(1, n):
         flat[d * cap : (d + 1) * cap, :] = rx[d].astype(f32)
     x_in[...] = flat[...].astype(bf16)
 
-    loads[2].wait()
-    step_rows = largest_part(wgu.shape[0], 256)
+    loads[10].wait()
+    step_rows = largest_part(wgu.shape[0], 480)
 
     def gate_up(i, carry):
         at = pl.ds(pl.multiple_of(i * step_rows, step_rows), step_rows)
@@ -411,7 +443,7 @@
         act[hidden_units:, :] = jnp.zeros((act.shape[0] - hidden_units, act.shape[1]), f32)
     activated = act[...].T[0:slots, 0:hidden_units].astype(bf16)
 
-    loads[3].wait()
+    loads[11].wait()
     down = jnp.dot(activated, wd[...], preferred_element_type=f32)
     left, right = down[:, 0:half], down[:, half:width]
     mine = jnp.where(h == 0, left, right)
@@ -440,9 +472,10 @@
 
     parts = slots // 16
     per_part = 16 // cap
-    for i in range(parts):
+    far_first = sorted(range(parts), key=lambda i: abs(2 * i + 1 - parts))
+    for i in far_first:
         exchange(i).start()
-    for i in range(parts):
+    for i in far_first:
         exchange(i).wait_recv()
         total = mine[i * 16 : (i + 1) * 16] + ex_rx[i * 16 : (i + 1) * 16, :].astype(f32)
         for j in range(per_part):
@@ -502,7 +535,6 @@
     units = w_down.shape[1]
     f32, bf16 = jnp.float32, jnp.bfloat16
     vmem = pl.BlockSpec(memory_space=pltpu.VMEM)
-    smem = pl.BlockSpec(memory_space=pltpu.SMEM)
     hbm = pl.BlockSpec(memory_space=pl.ANY)
     dma = pltpu.SemaphoreType.DMA
     wo = jnp.swapaxes(out_proj, 1, 2)
@@ -511,9 +543,17 @@
     return pl.pallas_call(
         functools.partial(fused_kernel, n),
         out_shape=jax.ShapeDtypeStruct((rows, half), bf16),
-        in_specs=[vmem, vmem, vmem, smem, smem, vmem, vmem, vmem, hbm, hbm, hbm, hbm],
+        in_specs=[hbm] * 12,
         out_specs=vmem,
         scratch_shapes=[
+            pltpu.SMEM(positions.shape, jnp.int32),
+            pltpu.SMEM(sink_logits.shape, f32),
+            pltpu.VMEM(queries.shape, bf16),
+            pltpu.VMEM(new_kv.shape, bf16),
+            pltpu.VMEM(route_ids.shape[::-1], jnp.int32),
+            pltpu.VMEM(route_weights.shape[::-1], jnp.int32),
+            pltpu.VMEM(residual.shape, bf16),
+            pltpu.VMEM(norm_gain.shape, f32),
             pltpu.VMEM(kv_cache.shape, bf16),
             pltpu.VMEM(wo.shape, bf16),
             pltpu.VMEM(wgu.shape, bf16),
@@ -534,7 +574,7 @@
             pltpu.VMEM((n, cap, half), bf16),
             pltpu.VMEM((n, cap, half), bf16),
             pltpu.VMEM((slots, half), f32),
-            dma((4,)),
+            dma((12,)),
             dma((2,)),
             dma((n,)),
             dma((n,)),
@@ -545,19 +585,19 @@
             dma((n,)),
         ],
         compiler_params=pltpu.CompilerParams(
-            collective_id=0, has_side_effects=True, vmem_limit_bytes=48 * 1024 * 1024
+            collective_id=0, has_side_effects=True, vmem_limit_bytes=60 * 1024 * 1024
         ),
     )(
-        residual,
+        positions,
+        sink_logits,
         queries,
         new_kv,
-        positions,
-        sink_logits,
-        norm_gain.reshape(1, width),
+        kv_cache,
+        wo,
         route_ids.T,
         route_weights.T,
-        kv_cache,
-        wo,
+        residual,
+        norm_gain,
         wgu,
         wd,
     )

time: 42.5 us -> 36.3 us (0.85)
  local copies, waits for them, and re-layouts: 7.99 us -> 1.42 us
  Pallas kernels: 34.1 us -> 34.7 us
    unnamed x17 -> x1, local copies, waits for them, and re-layouts: 7.27 us -> 1.42 us
    reshape x1 -> x0, local copies, waits for them, and re-layouts: 0.71 us -> none  [fused(): norm_gain.reshape(1, width)]
    pallas_call x1, Pallas kernels: 34.1 us -> 34.7 us  [fused(): pl.pallas_call(functools.partial(fused_kernel, n), out_shape=jax.ShapeDty...]
where the time goes in v2:
time: 36.3 us; the launch traced here: 36.2 us
  Pallas kernels  34.7 us (96%)
  local copies, waits for them, and re-layouts  1.42 us (4%)
    pallas_call x1, Pallas kernels, fused(): pl.pallas_call(functools.partial(fused_kernel, n), out_shape=jax.ShapeDty...  34.7 us
    unnamed x1, local copies, waits for them, and re-layouts  1.42 us

profile of v2, /device:TPU:0, one launch (start us, length us, event | category | flops | bytes accessed | tf_op | source)
XLA Modules:
  0.0 36.2 jit_solution(15057846208228183067)
XLA Ops:
  0.0 34.7 %shard_map.118 = bf16[16,1440]{1,0:T(8,128)(2,1)} custom-call(s32[16]{0:T(128)} %positions_hbm.1, f32[4,4]{1,0:T(4,128)} %sinks_hbm.1, bf16[16,4,256]{2,1,0:T(4,128)(2,1)} %queries_hbm.1, bf16[16,4,128]{2,1,0:T(4,128)(2,1)} %new_kv_hbm.1, bf16[16,4,128,128]{3,2,1,0:T(8,128)(2,1)} %kv_hbm.1, bf16[4,2880,256]{2,1,0:T(8,128)(2,1)} %bitcast.8, ...), custom_call_target="tpu_custom_call" | custom-call | tf_op jit(solution)/shard_map/pallas_call | solution.py:543
  34.7 1.4 %copy.14 = bf16[16,1440]{1,0:T(8,128)(2,1)} copy(bf16[16,1440]{1,0:T(8,128)(2,1)} %shard_map.118) | data formatting | bytes 92160
